TPU v7x, 128 devices: a whole 4x4x4 slice. The times are simulated.
128 devices in a mesh: ctx: 32 (over z, y_lo, x), head: 4 (over y_hi, core).
Axes of the slice: x: 4, y: 4 (y_hi: 2, y_lo: 2; y = y_hi * 2 + y_lo), z: 4, core: 2. Of those that a mesh axis runs over, the one named last changes fastest.
Arguments:
- queries: bfloat16 [16384, 2560], P('ctx', 'head'), may hold values from -6 to 6, as said below
- keys: bfloat16 [16384, 512], P('ctx', 'head'), may hold values from -6 to 6, as said below
- values: bfloat16 [16384, 512], P('ctx', 'head'), may hold values from -6 to 6
- lengths: int32 [32], replicated, may hold values from 1 to 1024, 16384 in all
- w_out: bfloat16 [5120, 2560], P(None, 'head'), may hold values from -0.125 to 0.125
- grad_y: bfloat16 [16384, 5120], P(('ctx', 'head')), may hold values from -6 to 6
Outputs:
- projected: bfloat16 [16384, 5120], P(('ctx', 'head'))
- grad_queries: bfloat16 [16384, 2560], P('ctx', 'head')
- grad_keys: bfloat16 [16384, 512], P('ctx', 'head')
- grad_values: bfloat16 [16384, 512], P('ctx', 'head')
- grad_weight: float32 [5120, 2560], P('ctx', 'head')
Inputs may be any that keep to these rules, and one draw needn't show every extreme that they name: `queries`: queries as drawn. `keys`: keys as drawn. The lengths sum to 16384; the longest is exactly 1024.
All inputs are finite; a program needn't handle non-finite values.
Results may differ from a plain program's by a relative error of at most 0.025.
Values may be sent and summed in bfloat16 or wider, within the bound.
A program may use at most 128 MiB of HBM per device.

v0:
```python
import math

import jax
import jax.numpy as jnp
from jax import lax
from jax.sharding import PartitionSpec as P

E = 128
WINDOW = 2


masked_score = -1e30


def passed_along(value, axis, steps):
    count = lax.axis_size(axis)
    first, last = (max(0, -steps), min(count, count - steps))
    return lax.ppermute(value, axis, [(source, source + steps) for source in range(first, last)])


def document_index(positions, doc_ends):
    return jnp.sum((positions[:, None] >= doc_ends[None, :]).astype(jnp.int32), axis=1)


def visibility(query_pos, key_pos, doc_ends):
    same_doc = (
        document_index(query_pos, doc_ends)[:, None] == document_index(key_pos, doc_ends)[None, :]
    )
    causal = key_pos[None, :] <= query_pos[:, None]
    return same_doc & causal & (key_pos[None, :] >= 0)


def pass_back(kv_pair):
    return passed_along(kv_pair, "ctx", 1)


def pass_home(grad_pair):
    return passed_along(grad_pair, "ctx", -1)


def on_device(queries, keys, values, lengths, w_out, grad_y):
    row_count = queries.shape[0]
    kv_groups = keys.shape[1] // E
    group_ratio = queries.shape[1] // keys.shape[1]
    score_scale = E ** (-0.5)
    span_index = lax.axis_index("ctx")
    doc_ends = jnp.cumsum(lengths)
    offsets = jnp.arange(row_count, dtype=jnp.int32)
    query_pos = span_index * row_count + offsets
    query_tiles = queries.reshape(row_count, kv_groups, group_ratio, E)
    cotangent = lax.all_gather(grad_y, "head", axis=0, tiled=True)
    upstream = jnp.dot(cotangent, w_out, preferred_element_type=jnp.float32).astype(jnp.bfloat16)
    upstream_tiles = upstream.reshape(row_count, kv_groups, group_ratio, E)
    kv_pair = jnp.stack((keys, values))
    kv_blocks = [kv_pair]
    for distance in range(WINDOW):
        kv_pair = pass_back(kv_pair)
        kv_blocks.append(kv_pair)
    visibility_all = [
        visibility(query_pos, (span_index - distance) * row_count + offsets, doc_ends)
        for distance in range(WINDOW + 1)
    ]
    score_blocks = []
    for distance in range(WINDOW + 1):

        def compute_scores(
            key_tiles=kv_blocks[distance][0].reshape(row_count, kv_groups, E),
            mask=visibility_all[distance],
        ):
            raw = (
                jnp.einsum(
                    "tgre,kge->grtk", query_tiles, key_tiles, preferred_element_type=jnp.float32
                )
                * score_scale
            )
            return jnp.where(mask, raw, masked_score)

        score_blocks.append(compute_scores())
    row_max = jnp.max(score_blocks[0], axis=-1, keepdims=True)
    for distance in range(1, WINDOW + 1):
        row_max = jnp.maximum(row_max, jnp.max(score_blocks[distance], axis=-1, keepdims=True))
    row_total = jnp.zeros_like(row_max)
    for distance in range(WINDOW + 1):
        row_total = row_total + jnp.sum(
            jnp.where(visibility_all[distance], jnp.exp(score_blocks[distance] - row_max), 0.0),
            axis=-1,
            keepdims=True,
        )
    log_total = row_max + jnp.log(row_total)
    weight_blocks = [
        jnp.where(
            visibility_all[distance], jnp.exp(score_blocks[distance] - log_total), 0.0
        ).astype(jnp.bfloat16)
        for distance in range(WINDOW + 1)
    ]
    tile_shape = (row_count, kv_groups, group_ratio, E)
    attended_sum = jnp.zeros(tile_shape, jnp.float32)
    for distance in range(WINDOW + 1):

        def compute_values(
            weights=weight_blocks[distance],
            value_tiles=kv_blocks[distance][1].reshape(row_count, kv_groups, E),
        ):
            return jnp.einsum(
                "grtk,kge->tgre", weights, value_tiles, preferred_element_type=jnp.float32
            )

        attended_sum = attended_sum + compute_values()
    attended = attended_sum.astype(jnp.bfloat16).reshape(row_count, -1)
    row_delta = jnp.sum(
        upstream_tiles.astype(jnp.float32) * attended.reshape(tile_shape).astype(jnp.float32),
        axis=-1,
    ).transpose(1, 2, 0)
    query_grad_sum = jnp.zeros(tile_shape, jnp.float32)
    grad_blocks = []
    for distance in range(WINDOW + 1):

        def compute_grads(
            weights=weight_blocks[distance],
            key_tiles=kv_blocks[distance][0].reshape(row_count, kv_groups, E),
            value_tiles=kv_blocks[distance][1].reshape(row_count, kv_groups, E),
        ):
            grad_prob = jnp.einsum(
                "tgre,kge->grtk", upstream_tiles, value_tiles, preferred_element_type=jnp.float32
            )
            grad_score = (weights.astype(jnp.float32) * (grad_prob - row_delta[..., None])).astype(
                jnp.bfloat16
            )
            query_part = jnp.einsum(
                "grtk,kge->tgre", grad_score, key_tiles, preferred_element_type=jnp.float32
            )
            key_part = (
                jnp.einsum(
                    "grtk,tgre->kge", grad_score, query_tiles, preferred_element_type=jnp.float32
                )
                * score_scale
            )
            value_part = jnp.einsum(
                "grtk,tgre->kge", weights, upstream_tiles, preferred_element_type=jnp.float32
            )
            return (
                query_part,
                jnp.stack((key_part.reshape(row_count, -1), value_part.reshape(row_count, -1))),
            )

        query_part, grad_pair = compute_grads()
        query_grad_sum = query_grad_sum + query_part
        grad_blocks.append(grad_pair)
    grad_queries = (query_grad_sum * score_scale).astype(jnp.bfloat16).reshape(row_count, -1)
    returning = grad_blocks[WINDOW]
    for distance in range(WINDOW - 1, -1, -1):
        returning = pass_home(returning) + grad_blocks[distance]
    grad_keys = returning[0].astype(jnp.bfloat16)
    grad_values = returning[1].astype(jnp.bfloat16)
    projected = lax.psum_scatter(
        lax.dot_general(
            attended, w_out, (((1,), (1,)), ((), ())), preferred_element_type=jnp.float32
        ),
        "head",
        scatter_dimension=0,
        tiled=True,
    ).astype(jnp.bfloat16)
    token_total = row_count * lax.axis_size("ctx")
    token_scale = 1.0 / math.sqrt(token_total)
    partial_grad = (
        lax.dot_general(
            cotangent, attended, (((0,), (0,)), ((), ())), preferred_element_type=jnp.float32
        )
        * token_scale
    )
    grad_weight = lax.psum_scatter(partial_grad, "ctx", scatter_dimension=0, tiled=True)
    return (projected, grad_queries, grad_keys, grad_values, grad_weight)


def solution(mesh):
    in_specs = (
        P("ctx", "head"),
        P("ctx", "head"),
        P("ctx", "head"),
        P(),
        P(None, "head"),
        P(("ctx", "head"), None),
    )
    out_specs = (
        P(("ctx", "head"), None),
        P("ctx", "head"),
        P("ctx", "head"),
        P("ctx", "head"),
        P("ctx", "head"),
    )
    return jax.shard_map(
        on_device, mesh=mesh, in_specs=in_specs, out_specs=out_specs, check_vma=False
    )
```

profile of v0, /device:TPU:16, one launch (start us, length us, event | category | flops | bytes accessed | tf_op | source)
XLA Modules:
  0.0 396.5 jit_solution(9207702825755981799)
XLA Ops:
  7.2 0.7 all-gather.2.cloned.1.call-update
  7.9 1.0 pad_maximum_fusion.1
  8.9 3.4 collective-permute-start
  12.4 0.7 copy.114
  13.2 0.1 reduce.7
  13.3 1.3 copy.115
  14.7 0.1 convert_reduce_fusion.1
  14.8 1.1 and_and_fusion.1
  15.9 1.9 fusion.6
  17.9 4.4 %collective-permute-start.1 = (bf16[2,512,128]{2,1,0:T(8,128)(2,1)S(1)}, bf16[2,512,128]{2,1,0:T(8,128)(2,1)S(1)}, u32[]{:S(2)}, u32[]{:S(2)}) collective-permute-start(bf16[2,512,128]{2,1,0:T(8,128)(2,1)S(1)} %collective-permute-done), channel_id=1, source_target_pairs={{0,4},{4,8},{8,12},{12,16},{16,20},{20,24},{24,28},{28,32},{32,36}... | collective-permute-start | bytes 786440 | tf_op jit(solution)/shard_map/ppermute | solution.py:18
  22.3 1.0 fusion.7
  23.3 3.6 collective-permute-done.1
  27.0 1.0 fusion.8
  28.0 4.0 %select_reduce_fusion.1 = (f32[5,512]{1,0:T(8,128)S(1)}, f32[5,512]{1,0:T(8,128)S(1)}, f32[5,512]{1,0:T(8,128)S(1)}) fusion(f32[512,512,5]{1,0,2:T(8,128)S(1)} %get-tuple-element.44, f32[5,512]{1,0:T(8,128)S(1)} %maximum_maximum_fusion, pred[512,512]{0,1:T(8,128)(4,1)S(1)} %get-tuple-element.36, f32[512,512,5]{1,0,2:T(8,128)S(1)} %get-tuple-element.40, ...), kind=kLoop, calls=%fused_computation.17 | loop fusion | flops 19653120 | bytes 16556032 | tf_op jit(solution)/shard_map/reduce_sum | solution.py:84
  32.1 5.1 %select_convert_fusion = (bf16[1,5,512,512]{2,3,1,0:T(8,128)(2,1)}, bf16[1,5,512,512]{2,3,1,0:T(8,128)(2,1)S(1)}, bf16[1,5,512,512]{2,3,1,0:T(8,128)(2,1)S(1)}) fusion(f32[512,512,5]{1,0,2:T(8,128)S(1)} %get-tuple-element.40, f32[5,512]{1,0:T(8,128)S(1)} %log_add_fusion, pred[512,512]{0,1:T(8,128)(4,1)S(1)} %get-tuple-element.37, ...), kind=kLoop, calls=%fused_computation.13 | loop fusion | flops 19660800 | bytes 24389632 | tf_op jit(solution)/shard_map/convert_element_type | solution.py:93
  37.1 0.6 fusion.31
  37.7 0.9 copy-done
  38.6 1.6 fusion.24
  40.2 19.0 %all-gather.2.cloned.1.call-done = bf16[512,5120]{1,0:T(8,128)(2,1)} async-done(((bf16[128,5120]{1,0:T(8,128)(2,1)}), bf16[512,5120]{1,0:T(8,128)(2,1)}) %all-gather.2.cloned.1.call-update) | async-done | bytes 5242896 | tf_op jit(solution)/shard_map/all_gather | solution.py:51
  59.3 8.6 %convolution_convert_fusion = bf16[512,640]{1,0:T(8,128)(2,1)S(1)} fusion(bf16[512,5120]{1,0:T(8,128)(2,1)} %all-gather.2.cloned.1.call-done, bf16[5120,640]{1,0:T(8,128)(2,1)} %param.10), kind=kOutput, calls=%fused_computation.46 | convolution fusion | flops 3355770880 | bytes 12451840 | tf_op jit(solution)/shard_map/dot_general | solution.py:52
  67.9 1.3 copy.128
  69.3 3.1 multiply_reduce_fusion
  72.3 9.7 %fusion.61 = f32[512,5120]{1,0:T(8,128)} fusion(bf16[512,640]{0,1:T(8,128)(2,1)S(1)} %bitcast.280, bf16[5120,640]{1,0:T(8,128)(2,1)} %param.10), kind=kOutput, calls=%fused_computation.92 | convolution fusion | flops 3355443200 | bytes 17694720 | tf_op jit(solution)/shard_map/dot_general | solution.py:156
  82.2 9.7 %multiply_bitcast_fusion = f32[5120,640]{0,1:T(8,128)} fusion(bf16[512,640]{0,1:T(8,128)(2,1)S(1)} %bitcast.281, bf16[512,5120]{1,0:T(8,128)(2,1)} %all-gather.2.cloned.1.call-done), kind=kOutput, calls=%fused_computation | convolution fusion | flops 3358720000 | bytes 19005440 | tf_op jit(solution)/shard_map/dot_general | solution.py:166
  91.9 15.0 %copy.185 = f32[5120,640]{1,0:T(8,128)} copy(f32[5120,640]{0,1:T(8,128)} %multiply_bitcast_fusion) | data formatting | bytes 26214400
  106.9 1.3 copy.125
  108.3 0.8 fusion.9
  109.2 0.9 copy-done.1
  110.0 0.8 fusion.10
  110.9 0.8 fusion.11
  111.8 0.6 convolution_bitcast_fusion
  112.3 0.5 convolution_add_fusion.1
  112.9 1.4 fusion.34
  114.3 2.2 copy.146
  116.4 2.9 fusion.50
  119.3 0.8 fusion.44
  120.2 1.4 collective-permute-start.2
  121.7 0.8 fusion.51
  122.5 0.8 fusion.41
  123.4 13.1 %collective-permute-done.2 = f32[2,512,128]{2,1,0:T(8,128)S(1)} collective-permute-done((f32[2,512,128]{2,1,0:T(8,128)S(1)}, f32[2,512,128]{2,1,0:T(8,128)S(1)}, u32[]{:S(2)}, u32[]{:S(2)}) %collective-permute-start.2) | collective-permute-done | bytes 524320 | tf_op jit(solution)/shard_map/ppermute | solution.py:18
  136.5 1.3 collective-permute-start.3
  137.8 0.8 fusion.52
  138.7 0.8 fusion.38
  139.5 12.4 %collective-permute-done.3 = f32[2,512,128]{2,1,0:T(8,128)S(1)} collective-permute-done((f32[2,512,128]{2,1,0:T(8,128)S(1)}, f32[2,512,128]{2,1,0:T(8,128)S(1)}, u32[]{:S(2)}, u32[]{:S(2)}) %collective-permute-start.3) | collective-permute-done | bytes 524320 | tf_op jit(solution)/shard_map/ppermute | solution.py:18
  151.9 0.7 slice_bitcast_fusion
  152.7 18.8 %reduce-scatter.5.cloned.1.call-done = f32[128,5120]{1,0:T(8,128)} async-done(((f32[512,5120]{1,0:T(8,128)}), f32[128,5120]{1,0:T(8,128)}) %reduce-scatter.5.cloned.1.call-update) | async-done | bytes 2621456 | tf_op jit(solution)/shard_map/reduce_scatter | solution.py:155
  171.5 3.0 convert_element_type.92
  174.4 215.6 %reduce-scatter.7.cloned.1.call-done = f32[160,640]{1,0:T(8,128)} async-done(((f32[5120,640]{1,0:T(8,128)}), f32[160,640]{1,0:T(8,128)}) %reduce-scatter.7.cloned.1.call-update) | async-done | bytes 409616
  (52 shorter events, 0.5 us)
Async XLA Ops:
  7.2 52.1 %all-gather.2.cloned.1.call-start = ((), (), s32[]{:S(2)}) async-start(), calls=%async_computation.3 | async-start | bytes 6553600 | tf_op jit(solution)/shard_map/all_gather | solution.py:51
  7.9 163.6 %reduce-scatter.5.cloned.1.call-start = ((), (), s32[]{:S(2)}) async-start(), calls=%async_computation.2 | async-start | bytes 13107200 | tf_op jit(solution)/shard_map/reduce_scatter | solution.py:155
  8.9 8.9 %collective-permute-start = (bf16[2,512,128]{2,1,0:T(8,128)(2,1)S(1)}, bf16[2,512,128]{2,1,0:T(8,128)(2,1)S(1)}, u32[]{:S(2)}, u32[]{:S(2)}) collective-permute-start(bf16[2,512,128]{2,1,0:T(8,128)(2,1)S(1)} %pad_maximum_fusion.1), channel_id=1, source_target_pairs={{0,4},{4,8},{8,12},{12,16},{16,20},{20,24},{24,28},{28,32},{32,36}... | collective-permute-start | bytes 786440 | tf_op jit(solution)/shard_map/ppermute | solution.py:18
  14.6 12.3 %copy-start.5 = (bf16[512,640]{0,1:T(8,128)(2,1)}, bf16[512,640]{0,1:T(8,128)(2,1)S(1)}, u32[]{:S(2)}) copy-start(bf16[512,640]{0,1:T(8,128)(2,1)S(1)} %copy.115) | copy-start | bytes 1966084
  17.9 19.8 %copy-start.17 = (bf16[2,512,128]{2,1,0:T(8,128)(2,1)}, bf16[2,512,128]{2,1,0:T(8,128)(2,1)S(1)}, u32[]{:S(2)}) copy-start(bf16[2,512,128]{2,1,0:T(8,128)(2,1)S(1)} %collective-permute-done) | copy-start | bytes 786436
  17.9 9.1 %collective-permute-start.1 = (bf16[2,512,128]{2,1,0:T(8,128)(2,1)S(1)}, bf16[2,512,128]{2,1,0:T(8,128)(2,1)S(1)}, u32[]{:S(2)}, u32[]{:S(2)}) collective-permute-start(bf16[2,512,128]{2,1,0:T(8,128)(2,1)S(1)} %collective-permute-done), channel_id=1, source_target_pairs={{0,4},{4,8},{8,12},{12,16},{16,20},{20,24},{24,28},{28,32},{32,36}... | collective-permute-start | bytes 786440 | tf_op jit(solution)/shard_map/ppermute | solution.py:18
  27.0 5.1 %copy-start.15 = (bf16[2,512,128]{2,1,0:T(8,128)(2,1)}, bf16[2,512,128]{2,1,0:T(8,128)(2,1)S(1)}, u32[]{:S(2)}) copy-start(bf16[2,512,128]{2,1,0:T(8,128)(2,1)S(1)} %collective-permute-done.1) | copy-start | bytes 786436
  32.1 5.1 %copy-start.13 = (bf16[512,128]{1,0:T(8,128)(2,1)S(1)}, bf16[512,128]{1,0:T(8,128)(2,1)}, u32[]{:S(2)}) copy-start(bf16[512,128]{1,0:T(8,128)(2,1)} %param.8) | copy-start | bytes 393220
  37.1 1.5 copy-start
  67.9 1.3 copy-start.12
  82.1 307.9 %reduce-scatter.7.cloned.1.call-start = ((), (), s32[]{:S(2)}) async-start(), calls=%async_computation.4 | async-start | bytes 13516800
  108.3 1.7 copy-start.1
  108.3 1.7 copy-start.18
  108.3 2.6 copy-start.3
  108.3 2.6 copy-start.16
  110.0 1.7 copy-start.7
  110.0 1.7 copy-start.14
  110.9 2.0 copy-start.9
  111.8 2.5 copy-start.11
  116.4 2.9 copy-start.4
  116.4 5.2 %copy-start.6 = (bf16[512,640]{0,1:T(8,128)(2,1)S(1)}, bf16[512,640]{0,1:T(8,128)(2,1)}, u32[]{:S(2)}) copy-start(bf16[512,640]{0,1:T(8,128)(2,1)} %copy-done.5) | copy-start | bytes 1966084
  116.4 5.2 %copy-start.10 = (bf16[5,512,512]{1,2,0:T(8,128)(2,1)S(1)}, bf16[5,512,512]{1,2,0:T(8,128)(2,1)}, u32[]{:S(2)}) copy-start(bf16[5,512,512]{1,2,0:T(8,128)(2,1)} %copy-done.9) | copy-start | bytes 7864324
  119.3 3.2 copy-start.2
  120.2 17.6 %copy-start.8 = (bf16[5,512,512]{1,2,0:T(8,128)(2,1)S(1)}, bf16[5,512,512]{1,2,0:T(8,128)(2,1)}, u32[]{:S(2)}) copy-start(bf16[5,512,512]{1,2,0:T(8,128)(2,1)} %copy-done.7) | copy-start | bytes 7864324
  120.2 16.2 %collective-permute-start.2 = (f32[2,512,128]{2,1,0:T(8,128)S(1)}, f32[2,512,128]{2,1,0:T(8,128)S(1)}, u32[]{:S(2)}, u32[]{:S(2)}) collective-permute-start(f32[2,512,128]{2,1,0:T(8,128)S(1)} %pad_maximum_fusion), channel_id=1, source_target_pairs={{4,0},{8,4},{12,8},{16,12},{20,16},{24,20},{28,24},{32,28},{36,32}... | collective-permute-start | bytes 1572872 | tf_op jit(solution)/shard_map/ppermute | solution.py:18
  136.5 15.4 %collective-permute-start.3 = (f32[2,512,128]{2,1,0:T(8,128)S(1)}, f32[2,512,128]{2,1,0:T(8,128)S(1)}, u32[]{:S(2)}, u32[]{:S(2)}) collective-permute-start(f32[2,512,128]{2,1,0:T(8,128)S(1)} %maximum_add_fusion), channel_id=1, source_target_pairs={{4,0},{8,4},{12,8},{16,12},{20,16},{24,20},{28,24},{32,28},{36,32}... | collective-permute-start | bytes 1572872 | tf_op jit(solution)/shard_map/ppermute | solution.py:18
Sparse Core Ops, SparseCore 0:
  9.7 49.5 all-gather.1
  82.2 89.1 reduce-scatter.4
  174.5 215.4 reduce-scatter.6
where the time goes:
time: 397 us
  waiting for transfers between devices  283 us (71%)
  matrix products  49.3 us (12%)
  local copies, waits for them, and re-layouts  24.5 us (6%)
  other arithmetic  14.6 us (4%)
  between operations  14.2 us (4%)
  starting transfers between devices  10.6 us (3%)
    unnamed x4, waiting for transfers between devices  216 us
    ppermute x4, waiting for transfers between devices, passed_along(): lax.ppermute(value, axis, [(source, source + steps) for source in range(f...  29.2 us
    unnamed x41, local copies, waits for them, and re-layouts  20.4 us
    all_gather x1, waiting for transfers between devices, on_device(): cotangent = lax.all_gather(grad_y, 'head', axis=0, tiled=True)  19 us
    reduce_scatter x1, waiting for transfers between devices, on_device(): lax.psum_scatter(lax.dot_general(attended, w_out, (((1,), (1,)), ((), ())...  18.8 us
    ppermute x4, starting transfers between devices, passed_along(): lax.ppermute(value, axis, [(source, source + steps) for source in range(f...  10.5 us
    dot_general x1, matrix products, on_device(): lax.dot_general(attended, w_out, (((1,), (1,)), ((), ())), preferred_elem...  9.75 us
    dot_general x1, matrix products, on_device(): lax.dot_general(cotangent, attended, (((0,), (0,)), ((), ())), preferred_...  9.72 us
  transfers between devices with their start and end apart: 7, of which 6 were waited for; matrix products, arithmetic and copies ran while one was open for 16% of the time, Pallas kernels for 0%

commit v1 on v0

v1 whole, which is shorter than its diff:
```python
import functools
import math

import jax
import jax.numpy as jnp
from jax import lax
from jax.experimental import pallas as pl
from jax.experimental.pallas import tpu as pltpu
from jax.sharding import PartitionSpec as P

E = 128
MESH = pl.DeviceIdType.MESH
F32 = jnp.float32
BF16 = jnp.bfloat16
NT = (((1,), (1,)), ((), ()))
TN = (((0,), (0,)), ((), ()))
NN = (((1,), (0,)), ((), ()))
RATIO = 5
ROWS = 512
COLS = RATIO * E
WIDTH = 9 * E
MODEL = 5120
GROUP = 640
PIECE = 160
MASKED = -1e30
Z_STEPS = (2, 1, 3, 0)


def dot(a, b, dims):
    return lax.dot_general(a, b, dims, preferred_element_type=F32)


def stack_heads(ref, first):
    return jnp.concatenate(
        [ref[pl.ds(first, E), r * E : (r + 1) * E] for r in range(RATIO)], axis=0
    )


def kernel(
    q_hbm,
    k_hbm,
    v_hbm,
    lengths,
    w_hbm,
    gy_hbm,
    proj_out,
    dq_out,
    dk_out,
    dv_out,
    gw_out,
    q,
    kw,
    vw,
    w,
    cot,
    att,
    up,
    up_acc,
    probs,
    scores,
    dk_acc,
    dv_acc,
    home_send,
    home_recv,
    part,
    core_recv,
    y_send,
    y_recv,
    stage,
    ax_recv,
    az_send,
    az_recv,
    bz_recv,
    bx_send,
    bx_recv,
    l_send,
    l_recv,
    local_sem,
    kv_ss,
    kv_rs,
    own_ss,
    own_rs,
    ag_ss,
    ag_rs,
    fw_ss,
    fw_rs,
    home_ss,
    home_rs,
    pc_ss,
    pc_rs,
    py_ss,
    py_rs,
    ax_ss,
    ax_rs,
    az_ss,
    az_rs,
    bz_ss,
    bz_rs,
    bx_ss,
    bx_rs,
    l_ss,
    l_rs,
):
    c = lax.axis_index("ctx")
    h = lax.axis_index("head")
    z, yl, x = c // 8, (c // 4) % 2, c % 4
    core, yh = h % 2, h // 2
    h_core = h + 1 - 2 * core
    h_far = (h + 2) % 4
    core_dev = (c, h_core)
    far_dev = (c, h_far)
    lo_dev = (c + 4 - 8 * yl, h)

    def x_dev(step):
        return (c - x + (x + step) % 4, h)

    def z_dev(step):
        return ((c + 8 * step) % 32, h)

    def c_dev(step):
        return ((c + step + 32) % 32, h)

    sends = []

    def send(src, dst, ss, rs, device):
        copy = pltpu.make_async_remote_copy(
            src_ref=src, dst_ref=dst, send_sem=ss, recv_sem=rs, device_id=device, device_id_type=MESH
        )
        copy.start()
        sends.append(copy)
        return copy

    def rows_of(head):
        return pl.ds(pl.multiple_of(head * 128, 128), 128)

    own_rows = rows_of(h)
    far_rows = rows_of(h_far)

    def group_cols(n):
        first = (((z + Z_STEPS[n // 2]) % 4) * 2 + n % 2) * GROUP
        return pl.ds(pl.multiple_of(first, 128), GROUP)

    local = []
    for index, (src, dst) in enumerate(
        (
            (q_hbm, q),
            (k_hbm, kw.at[1024:1536]),
            (v_hbm, vw.at[1024:1536]),
            (gy_hbm, cot.at[own_rows]),
            (w_hbm, w),
        )
    ):
        copy = pltpu.make_async_copy(src, dst, local_sem.at[index])
        copy.start()
        local.append(copy)

    barrier = pltpu.get_barrier_semaphore()
    peers = [core_dev, far_dev, lo_dev]
    peers += [x_dev(s) for s in (1, 2, 3)] + [z_dev(s) for s in (1, 2, 3)]
    peers += [c_dev(s) for s in (1, 2, -1, -2)]
    for peer in peers:
        pl.semaphore_signal(barrier, inc=1, device_id=peer, device_id_type=MESH)
    pl.semaphore_wait(barrier, len(peers))

    kv = []
    for src, dst, base in ((k_hbm, kw, 0), (v_hbm, vw, 2)):
        for step in (1, 2):
            slot = base + step - 1
            kv.append(
                send(
                    src,
                    dst.at[(2 - step) * 512 : (3 - step) * 512],
                    kv_ss.at[slot],
                    kv_rs.at[slot],
                    c_dev(step),
                )
            )
    gathers = []
    for n in range(8):
        cols = group_cols(n)
        gathers.append(
            send(gy_hbm.at[:, cols], cot.at[own_rows, cols], ag_ss.at[n], ag_rs.at[n], far_dev)
        )
    own_copy = send(gy_hbm, cot.at[own_rows], own_ss.at[0], own_rs.at[0], core_dev)

    scale = E ** (-0.5)
    log2e = scale * math.log2(math.e)

    def mask_bias(tile, chunk):
        t = c * ROWS + tile * E + lax.broadcasted_iota(jnp.int32, (1, E), 1)
        start = jnp.zeros((1, E), jnp.int32)
        run = jnp.int32(0)
        for d in range(32):
            run = run + lengths[d]
            start = jnp.where(t >= run, run, start)
        return t, start

    def visible(t, start, tile, chunk):
        j = (c - 2) * ROWS + tile * E + chunk * E + lax.broadcasted_iota(jnp.int32, (E, E), 0)
        bias = jnp.where((j >= start) & (j <= t), 0.0, MASKED)
        return jnp.concatenate([bias] * RATIO, axis=1)

    local[0].wait()
    local[1].wait()
    kv[0].wait_recv()
    kv[1].wait_recv()

    def weigh(tile, carry):
        first = pl.multiple_of(tile * E, E)
        t, start = mask_bias(tile, 0)
        qt = stack_heads(q, first)
        scores[...] = dot(kw[pl.ds(first, WIDTH), :], qt, NT)

        def largest(chunk, top):
            rows = pl.ds(pl.multiple_of(chunk * E, E), E)
            s = scores[rows, :] + visible(t, start, tile, chunk)
            scores[rows, :] = s
            return jnp.maximum(top, jnp.max(s.reshape(16, 8, COLS), axis=0))

        top = lax.fori_loop(0, 9, largest, jnp.full((8, COLS), MASKED, F32))
        top = jnp.max(top, axis=0, keepdims=True)

        def powers(chunk, total):
            rows = pl.ds(pl.multiple_of(chunk * E, E), E)
            p = jnp.exp2((scores[rows, :] - top) * log2e)
            scores[rows, :] = p
            return total + jnp.sum(p.reshape(16, 8, COLS), axis=0)

        total = lax.fori_loop(0, 9, powers, jnp.zeros((8, COLS), F32))
        inverse = 1.0 / jnp.sum(total, axis=0, keepdims=True)

        def normal(chunk, carry):
            rows = pl.ds(pl.multiple_of(chunk * E, E), E)
            probs[tile, rows, :] = (scores[rows, :] * inverse).astype(BF16)
            return carry

        lax.fori_loop(0, 9, normal, 0)
        return carry

    lax.fori_loop(0, 4, weigh, 0)
    local[2].wait()
    kv[2].wait_recv()
    kv[3].wait_recv()

    def attend(tile, carry):
        first = pl.multiple_of(tile * E, E)
        out = dot(vw[pl.ds(first, WIDTH), :], probs[tile], TN)
        for r in range(RATIO):
            att[pl.ds(first, E), r * E : (r + 1) * E] = out[:, r * E : (r + 1) * E].T.astype(BF16)
        return carry

    lax.fori_loop(0, 4, attend, 0)

    forwards = []

    def forward(n):
        gathers[n].wait_recv()
        cols = group_cols(n)
        ref = cot.at[far_rows, cols]
        forwards.append(send(ref, ref, fw_ss.at[n], fw_rs.at[n], core_dev))

    ax, bz = {}, {}

    def weight_group(n):
        forwards[n].wait_recv()
        step = Z_STEPS[n // 2]
        stage[n] = dot(cot[:, group_cols(n)], att[...], TN).astype(BF16)
        if n % 2 == 0:
            for dx in (2, 1, 3):
                first = pl.multiple_of(((x + dx) % 4) * PIECE, 32)
                slot = (n // 2) * 3 + dx - 1
                ax[n // 2, dx] = send(
                    stage.at[n, pl.ds(first, PIECE)],
                    ax_recv.at[slot],
                    ax_ss.at[slot],
                    ax_rs.at[slot],
                    x_dev(dx),
                )
        elif step:
            bz[step] = send(
                stage.at[n],
                bz_recv.at[step - 1],
                bz_ss.at[step - 1],
                bz_rs.at[step - 1],
                z_dev(step),
            )

    local[3].wait()
    own_copy.wait_recv()
    for n in range(4):
        forward(n)
    for n in range(4):
        weight_group(n)

    local[4].wait()

    def project(n, carry):
        first = pl.multiple_of(n * GROUP, 128)
        part[:, pl.ds(first, GROUP)] = dot(att[...], w[pl.ds(first, GROUP), :], NT).astype(BF16)
        return carry

    lax.fori_loop(0, 8, project, 0)
    to_core = {}
    for far in (1, 0):
        head = (h_core + 2 * far) % 4
        to_core[far] = send(
            part.at[rows_of(head)], core_recv.at[far], pc_ss.at[far], pc_rs.at[far], core_dev
        )
    for n in range(4, 6):
        forward(n)
    for n in range(4, 6):
        weight_group(n)
    to_core[1].wait_recv()
    to_far = []
    for n in range(4):
        cols = pl.ds(n * 1280, 1280)
        y_send[:, cols] = (part[far_rows, cols].astype(F32) + core_recv[1, :, cols].astype(F32)).astype(
            BF16
        )
        to_far.append(send(y_send.at[:, cols], y_recv.at[:, cols], py_ss.at[n], py_rs.at[n], far_dev))
    for n in range(6, 8):
        forward(n)
    for n in range(6, 8):
        weight_group(n)

    up_acc[...] = jnp.zeros_like(up_acc)

    def raise_up(n, carry):
        first = pl.multiple_of(n * GROUP, 128)
        up_acc[...] += dot(cot[:, pl.ds(first, GROUP)], w[pl.ds(first, GROUP), :], NN)
        return carry

    lax.fori_loop(0, 8, raise_up, 0)
    up[...] = up_acc[...].astype(BF16)

    az = {}

    def sum_x(index):
        step = Z_STEPS[index]
        first = pl.multiple_of(x * PIECE, 32)
        total = stage[2 * index, pl.ds(first, PIECE), :].astype(F32)
        for dx in (1, 2, 3):
            ax[index, dx].wait_recv()
            total = total + ax_recv[index * 3 + dx - 1].astype(F32)
        if step:
            az_send[step - 1] = total.astype(BF16)
            az[step] = send(
                az_send.at[step - 1],
                az_recv.at[step - 1],
                az_ss.at[step - 1],
                az_rs.at[step - 1],
                z_dev(step),
            )
        return total

    sum_x(0)
    sum_x(1)

    dk_acc[...] = jnp.zeros_like(dk_acc)
    dv_acc[...] = jnp.zeros_like(dv_acc)

    def backward(tile, carry):
        first = pl.multiple_of(tile * E, E)
        window = pl.ds(first, WIDTH)
        up_t = stack_heads(up, first)
        delta = []
        for r in range(RATIO):
            cols = slice(r * E, (r + 1) * E)
            prod = up[pl.ds(first, E), cols].astype(F32) * att[pl.ds(first, E), cols].astype(F32)
            delta.append(jnp.sum(prod.T, axis=0, keepdims=True))
        delta = jnp.concatenate(delta, axis=1)
        scores[...] = dot(vw[window, :], up_t, NT)
        dv_acc[window, :] += dot(probs[tile], up_t, NN)

        def grad(chunk, carry):
            rows = pl.ds(pl.multiple_of(chunk * E, E), E)
            weight = probs[tile, rows, :].astype(F32)
            probs[tile, rows, :] = (weight * (scores[rows, :] - delta)).astype(BF16)
            return carry

        lax.fori_loop(0, 9, grad, 0)
        dk_acc[window, :] += dot(probs[tile], stack_heads(q, first), NN)
        dq = dot(kw[window, :], probs[tile], TN) * scale
        for r in range(RATIO):
            dq_out[pl.ds(first, E), r * E : (r + 1) * E] = dq[:, r * E : (r + 1) * E].T.astype(BF16)
        return carry

    lax.fori_loop(0, 4, backward, 0)
    homes = []
    for index, acc in enumerate((dk_acc, dv_acc)):
        factor = scale if index == 0 else 1.0
        for step in (2, 1):
            slot = index * 2 + step - 1
            home_send[slot] = (acc[(2 - step) * 512 : (3 - step) * 512, :] * factor).astype(BF16)
            homes.append(
                send(
                    home_send.at[slot],
                    home_recv.at[slot],
                    home_ss.at[slot],
                    home_rs.at[slot],
                    c_dev(-step),
                )
            )

    sum_x(2)
    total_a = sum_x(3)
    for dz in (1, 2, 3):
        bz[dz].wait_recv()

    def sum_z(dx):
        rows = pl.ds(pl.multiple_of(((x + dx) % 4) * PIECE, 32), PIECE)
        total = stage[7, rows, :].astype(F32)
        for dz in (1, 2, 3):
            total = total + bz_recv[dz - 1, rows, :].astype(F32)
        return total

    bx = {}
    for dx in (2, 1, 3):
        bx_send[dx - 1] = sum_z(dx).astype(BF16)
        bx[dx] = send(
            bx_send.at[dx - 1], bx_recv.at[dx - 1], bx_ss.at[dx - 1], bx_rs.at[dx - 1], x_dev(dx)
        )
    total_b = sum_z(0)
    for dz in (1, 2, 3):
        az[dz].wait_recv()
        total_a = total_a + az_recv[dz - 1].astype(F32)
    for dx in (1, 2, 3):
        bx[dx].wait_recv()
        total_b = total_b + bx_recv[dx - 1].astype(F32)
    lower = yl == 0
    l_send[...] = jnp.where(lower, total_b, total_a).astype(BF16)
    last = send(l_send, l_recv, l_ss.at[0], l_rs.at[0], lo_dev)

    for copy in homes:
        copy.wait_recv()
    for index, (acc, out) in enumerate(((dk_acc, dk_out), (dv_acc, dv_out))):
        factor = scale if index == 0 else 1.0
        total = acc[1024:1536, :] * factor
        for step in (1, 2):
            total = total + home_recv[index * 2 + step - 1].astype(F32)
        out[...] = total.astype(BF16)

    to_core[0].wait_recv()
    for n in range(4):
        cols = pl.ds(n * 1280, 1280)
        to_far[n].wait_recv()
        proj_out[:, cols] = (
            part[own_rows, cols].astype(F32)
            + core_recv[0, :, cols].astype(F32)
            + y_recv[:, cols].astype(F32)
        ).astype(BF16)

    last.wait_recv()
    mine = jnp.where(lower, total_a, total_b)
    gw_out[...] = (mine + l_recv[...].astype(F32)) * (1.0 / 128.0)
    for copy in sends:
        copy.wait_send()


def on_device(queries, keys, values, lengths, w_out, grad_y):
    hbm = pl.BlockSpec(memory_space=pl.ANY)
    vmem = pl.BlockSpec(memory_space=pltpu.VMEM)
    dma = lambda n: pltpu.SemaphoreType.DMA((n,))
    return pl.pallas_call(
        kernel,
        out_shape=(
            jax.ShapeDtypeStruct((128, MODEL), BF16),
            jax.ShapeDtypeStruct((ROWS, COLS), BF16),
            jax.ShapeDtypeStruct((ROWS, E), BF16),
            jax.ShapeDtypeStruct((ROWS, E), BF16),
            jax.ShapeDtypeStruct((PIECE, COLS), F32),
        ),
        in_specs=[hbm, hbm, hbm, pl.BlockSpec(memory_space=pltpu.SMEM), hbm, hbm],
        out_specs=(vmem,) * 5,
        scratch_shapes=[
            pltpu.VMEM((ROWS, COLS), BF16),
            pltpu.VMEM((3 * ROWS, E), BF16),
            pltpu.VMEM((3 * ROWS, E), BF16),
            pltpu.VMEM((MODEL, COLS), BF16),
            pltpu.VMEM((ROWS, MODEL), BF16),
            pltpu.VMEM((ROWS, COLS), BF16),
            pltpu.VMEM((ROWS, COLS), BF16),
            pltpu.VMEM((ROWS, COLS), F32),
            pltpu.VMEM((4, WIDTH, COLS), BF16),
            pltpu.VMEM((WIDTH, COLS), F32),
            pltpu.VMEM((3 * ROWS, E), F32),
            pltpu.VMEM((3 * ROWS, E), F32),
            pltpu.VMEM((4, ROWS, E), BF16),
            pltpu.VMEM((4, ROWS, E), BF16),
            pltpu.VMEM((ROWS, MODEL), BF16),
            pltpu.VMEM((2, 128, MODEL), BF16),
            pltpu.VMEM((128, MODEL), BF16),
            pltpu.VMEM((128, MODEL), BF16),
            pltpu.VMEM((8, GROUP, COLS), BF16),
            pltpu.VMEM((12, PIECE, COLS), BF16),
            pltpu.VMEM((3, PIECE, COLS), BF16),
            pltpu.VMEM((3, PIECE, COLS), BF16),
            pltpu.VMEM((3, GROUP, COLS), BF16),
            pltpu.VMEM((3, PIECE, COLS), BF16),
            pltpu.VMEM((3, PIECE, COLS), BF16),
            pltpu.VMEM((PIECE, COLS), BF16),
            pltpu.VMEM((PIECE, COLS), BF16),
            dma(5),
            dma(4),
            dma(4),
            dma(1),
            dma(1),
            dma(8),
            dma(8),
            dma(8),
            dma(8),
            dma(4),
            dma(4),
            dma(2),
            dma(2),
            dma(4),
            dma(4),
            dma(12),
            dma(12),
            dma(3),
            dma(3),
            dma(3),
            dma(3),
            dma(3),
            dma(3),
            dma(1),
            dma(1),
        ],
        compiler_params=pltpu.CompilerParams(
            collective_id=0, has_side_effects=True, vmem_limit_bytes=63 << 20
        ),
    )(queries, keys, values, lengths, w_out, grad_y)


def solution(mesh):
    in_specs = (
        P("ctx", "head"),
        P("ctx", "head"),
        P("ctx", "head"),
        P(),
        P(None, "head"),
        P(("ctx", "head"), None),
    )
    out_specs = (
        P(("ctx", "head"), None),
        P("ctx", "head"),
        P("ctx", "head"),
        P("ctx", "head"),
        P("ctx", "head"),
    )
    return jax.shard_map(
        on_device, mesh=mesh, in_specs=in_specs, out_specs=out_specs, check_vma=False
    )
```

time: 397 us -> 105 us (0.26)
  the two profiles are of different devices: /device:TPU:16 before, /device:TPU:15 now
where the time goes in v1:
time: 105 us; the launch traced here: 104 us
  Pallas kernels  98 us (93%)
  local copies, waits for them, and re-layouts  5.59 us (5%)
    pallas_call x1, Pallas kernels, on_device(): pl.pallas_call(kernel, out_shape=(jax.ShapeDtypeStruct((128, MODEL), BF16...  98 us
    unnamed x13, local copies, waits for them, and re-layouts  5.59 us

profile of v1, /device:TPU:15, one launch (start us, length us, event | category | flops | bytes accessed | tf_op | source)
XLA Modules:
  0.0 104.2 jit_solution(12969565602991569349)
XLA Ops:
  0.6 98.0 %shard_map.101 = (bf16[128,5120]{1,0:T(8,128)(2,1)}, bf16[512,640]{1,0:T(8,128)(2,1)}, bf16[512,128]{1,0:T(8,128)(2,1)}, bf16[512,128]{1,0:T(8,128)(2,1)}, f32[160,640]{1,0:T(8,128)}) custom-call(bf16[512,640]{1,0:T(8,128)(2,1)} %q_hbm.1, bf16[512,128]{1,0:T(8,128)(2,1)} %k_hbm.1, bf16[512,128]{1,0:T(8,128)(2,1)} %v_hbm.1, s32[32]{0:T(128)} %lengths.1, ...), custom_call_target="tpu_custom_call" | custom-call | tf_op jit(solution)/shard_map/pallas_call | solution.py:464
  98.6 0.0 copy-start
  98.7 2.5 %copy.16 = bf16[128,5120]{1,0:T(8,128)(2,1)} copy(bf16[128,5120]{1,0:T(8,128)(2,1)} %get-tuple-element.10) | data formatting | bytes 2621440
  101.2 0.0 copy-done
  101.2 0.0 copy-start.3
  101.2 0.0 copy-start.2
  101.2 0.0 copy-start.1
  101.2 0.8 copy.17
  102.0 0.2 copy-done.3
  102.2 0.7 copy.18
  102.8 0.0 copy-done.2
  102.8 0.7 copy.19
  103.5 0.0 copy-done.1
  103.5 0.8 copy.20
Async XLA Ops:
  98.6 2.5 %copy-start = (bf16[512,640]{1,0:T(8,128)(2,1)S(1)}, bf16[512,640]{1,0:T(8,128)(2,1)}, u32[]{:S(2)}) copy-start(bf16[512,640]{1,0:T(8,128)(2,1)} %get-tuple-element.11) | copy-start | bytes 1966084
  101.2 1.0 copy-start.3
  101.2 1.7 %copy-start.2 = (bf16[512,128]{1,0:T(8,128)(2,1)S(1)}, bf16[512,128]{1,0:T(8,128)(2,1)}, u32[]{:S(2)}) copy-start(bf16[512,128]{1,0:T(8,128)(2,1)} %get-tuple-element.13) | copy-start | bytes 393220
  101.2 2.3 %copy-start.1 = (f32[160,640]{1,0:T(8,128)S(1)}, f32[160,640]{1,0:T(8,128)}, u32[]{:S(2)}) copy-start(f32[160,640]{1,0:T(8,128)} %get-tuple-element.14) | copy-start | bytes 1228804

commit v2 on v1

--- a/solution.py
+++ b/solution.py
@@ -43,6 +43,11 @@
     lengths,
     w_hbm,
     gy_hbm,
+    proj_hbm,
+    dq_hbm,
+    dk_hbm,
+    dv_hbm,
+    gw_hbm,
     proj_out,
     dq_out,
     dk_out,
@@ -51,6 +56,7 @@
     q,
     kw,
     vw,
+    kv_relay,
     w,
     cot,
     att,
@@ -76,8 +82,12 @@
     l_send,
     l_recv,
     local_sem,
+    out_sem,
     kv_ss,
     kv_rs,
+    kr_ss,
+    kr_rs,
+    kf_ss,
     own_ss,
     own_rs,
     ag_ss,
@@ -86,6 +96,8 @@
     fw_rs,
     home_ss,
     home_rs,
+    hp_ss,
+    hp_rs,
     pc_ss,
     pc_rs,
     py_ss,
@@ -122,10 +134,13 @@
 
     sends = []
 
+    def remote(src, dst, ss, rs, device):
+        return pltpu.make_async_remote_copy(
+            src_ref=src, dst_ref=dst, send_sem=ss, recv_sem=rs, device_id=device, device_id_type=MESH
+        )
+
     def send(src, dst, ss, rs, device):
-        copy = pltpu.make_async_remote_copy(
-            src_ref=src, dst_ref=dst, send_sem=ss, recv_sem=rs, device_id=device, device_id_type=MESH
-        )
+        copy = remote(src, dst, ss, rs, device)
         copy.start()
         sends.append(copy)
         return copy
@@ -157,24 +172,54 @@
     barrier = pltpu.get_barrier_semaphore()
     peers = [core_dev, far_dev, lo_dev]
     peers += [x_dev(s) for s in (1, 2, 3)] + [z_dev(s) for s in (1, 2, 3)]
-    peers += [c_dev(s) for s in (1, 2, -1, -2)]
+    peers += [c_dev(s) for s in (1, 2, 3, 4, -1, -2, -3, -4)]
     for peer in peers:
         pl.semaphore_signal(barrier, inc=1, device_id=peer, device_id_type=MESH)
     pl.semaphore_wait(barrier, len(peers))
 
-    kv = []
-    for src, dst, base in ((k_hbm, kw, 0), (v_hbm, vw, 2)):
-        for step in (1, 2):
-            slot = base + step - 1
-            kv.append(
-                send(
-                    src,
-                    dst.at[(2 - step) * 512 : (3 - step) * 512],
-                    kv_ss.at[slot],
-                    kv_rs.at[slot],
-                    c_dev(step),
-                )
+    near, far, relays, hops = [], [], [], []
+    for index, (src, dst) in enumerate(((k_hbm, kw), (v_hbm, vw))):
+        near_dst, far_dst, relay = dst.at[512:1024], dst.at[0:512], kv_relay.at[index]
+        near_sem, far_sem = kv_rs.at[2 * index], kv_rs.at[2 * index + 1]
+        near.append(remote(src, near_dst, kv_ss.at[2 * index], near_sem, c_dev(1)))
+        far.append(remote(src, far_dst, kv_ss.at[2 * index + 1], far_sem, c_dev(2)))
+        relays.append(remote(src, relay, kr_ss.at[index], kr_rs.at[index], c_dev(4)))
+        hops.append(
+            (
+                remote(relay, near_dst, kf_ss.at[2 * index], near_sem, c_dev(-3)),
+                remote(relay, far_dst, kf_ss.at[2 * index + 1], far_sem, c_dev(-2)),
             )
+        )
+
+    @pl.when(x >= 2)
+    def _():
+        relays[0].start()
+        relays[1].start()
+
+    for index in (0, 1):
+
+        @pl.when(x != 3)
+        def _():
+            near[index].start()
+
+        @pl.when(x < 2)
+        def _():
+            far[index].start()
+
+    def pass_block(index):
+        @pl.when(x >= 2)
+        def _():
+            relays[index].wait_recv()
+            hops[index][1].start()
+
+        @pl.when(x == 3)
+        def _():
+            hops[index][0].start()
+
+    def receive_block(index):
+        near[index].wait_recv()
+        far[index].wait_recv()
+
     gathers = []
     for n in range(8):
         cols = group_cols(n)
@@ -202,8 +247,9 @@
 
     local[0].wait()
     local[1].wait()
-    kv[0].wait_recv()
-    kv[1].wait_recv()
+    pass_block(0)
+    pass_block(1)
+    receive_block(0)
 
     def weigh(tile, carry):
         first = pl.multiple_of(tile * E, E)
@@ -239,8 +285,7 @@
 
     lax.fori_loop(0, 4, weigh, 0)
     local[2].wait()
-    kv[2].wait_recv()
-    kv[3].wait_recv()
+    receive_block(1)
 
     def attend(tile, carry):
         first = pl.multiple_of(tile * E, E)
@@ -261,16 +306,18 @@
 
     ax, bz = {}, {}
 
+    def block_rows(step, first, count):
+        return pl.ds(pl.multiple_of(((x + step) % 4) * PIECE + first, 16), count)
+
     def weight_group(n):
         forwards[n].wait_recv()
         step = Z_STEPS[n // 2]
         stage[n] = dot(cot[:, group_cols(n)], att[...], TN).astype(BF16)
         if n % 2 == 0:
             for dx in (2, 1, 3):
-                first = pl.multiple_of(((x + dx) % 4) * PIECE, 32)
                 slot = (n // 2) * 3 + dx - 1
                 ax[n // 2, dx] = send(
-                    stage.at[n, pl.ds(first, PIECE)],
+                    stage.at[n, block_rows(dx, 0, PIECE)],
                     ax_recv.at[slot],
                     ax_ss.at[slot],
                     ax_rs.at[slot],
@@ -285,6 +332,12 @@
                 z_dev(step),
             )
 
+    def raise_up(pair):
+        first = pl.multiple_of(((z + Z_STEPS[pair]) % 4) * 2 * GROUP, 128)
+        columns = pl.ds(first, 2 * GROUP)
+        more = dot(cot[:, columns], w[columns, :], NN)
+        up_acc[...] = more if pair == 0 else up_acc[...] + more
+
     local[3].wait()
     own_copy.wait_recv()
     for n in range(4):
@@ -301,44 +354,43 @@
 
     lax.fori_loop(0, 8, project, 0)
     to_core = {}
-    for far in (1, 0):
-        head = (h_core + 2 * far) % 4
-        to_core[far] = send(
-            part.at[rows_of(head)], core_recv.at[far], pc_ss.at[far], pc_rs.at[far], core_dev
-        )
+    for side in (1, 0):
+        head = (h_core + 2 * side) % 4
+        to_core[side] = send(
+            part.at[rows_of(head)], core_recv.at[side], pc_ss.at[side], pc_rs.at[side], core_dev
+        )
+    raise_up(0)
+    raise_up(1)
     for n in range(4, 6):
         forward(n)
     for n in range(4, 6):
         weight_group(n)
     to_core[1].wait_recv()
     to_far = []
-    for n in range(4):
+
+    def sum_core(n):
         cols = pl.ds(n * 1280, 1280)
         y_send[:, cols] = (part[far_rows, cols].astype(F32) + core_recv[1, :, cols].astype(F32)).astype(
             BF16
         )
         to_far.append(send(y_send.at[:, cols], y_recv.at[:, cols], py_ss.at[n], py_rs.at[n], far_dev))
+
+    sum_core(0)
+    raise_up(2)
     for n in range(6, 8):
         forward(n)
+    for n in range(1, 4):
+        sum_core(n)
     for n in range(6, 8):
         weight_group(n)
-
-    up_acc[...] = jnp.zeros_like(up_acc)
-
-    def raise_up(n, carry):
-        first = pl.multiple_of(n * GROUP, 128)
-        up_acc[...] += dot(cot[:, pl.ds(first, GROUP)], w[pl.ds(first, GROUP), :], NN)
-        return carry
-
-    lax.fori_loop(0, 8, raise_up, 0)
+    raise_up(3)
     up[...] = up_acc[...].astype(BF16)
 
     az = {}
 
     def sum_x(index):
         step = Z_STEPS[index]
-        first = pl.multiple_of(x * PIECE, 32)
-        total = stage[2 * index, pl.ds(first, PIECE), :].astype(F32)
+        total = stage[2 * index, block_rows(0, 0, PIECE), :].astype(F32)
         for dx in (1, 2, 3):
             ax[index, dx].wait_recv()
             total = total + ax_recv[index * 3 + dx - 1].astype(F32)
@@ -354,10 +406,20 @@
         return total
 
     sum_x(0)
-    sum_x(1)
 
     dk_acc[...] = jnp.zeros_like(dk_acc)
     dv_acc[...] = jnp.zeros_like(dv_acc)
+
+    def home_piece(index, tile):
+        rows = pl.ds(pl.multiple_of(tile * E, E), E)
+        slot = index * 2 + 1
+        return remote(
+            home_send.at[slot, rows],
+            home_recv.at[slot, rows],
+            hp_ss.at[index, tile],
+            hp_rs.at[index, tile],
+            c_dev(-2),
+        )
 
     def backward(tile, carry):
         first = pl.multiple_of(tile * E, E)
@@ -380,35 +442,50 @@
 
         lax.fori_loop(0, 9, grad, 0)
         dk_acc[window, :] += dot(probs[tile], stack_heads(q, first), NN)
+        rows = pl.ds(first, E)
+        home_send[1, rows] = (dk_acc[rows, :] * scale).astype(BF16)
+        home_send[3, rows] = dv_acc[rows, :].astype(BF16)
+        for index in (0, 1):
+            home_piece(index, tile).start()
         dq = dot(kw[window, :], probs[tile], TN) * scale
         for r in range(RATIO):
             dq_out[pl.ds(first, E), r * E : (r + 1) * E] = dq[:, r * E : (r + 1) * E].T.astype(BF16)
         return carry
 
-    lax.fori_loop(0, 4, backward, 0)
-    homes = []
+    lax.fori_loop(0, 2, backward, 0)
+    sum_x(1)
+    lax.fori_loop(2, 4, backward, 0)
+    homes = [home_piece(index, tile) for index in (0, 1) for tile in range(4)]
+    sends.extend(homes)
     for index, acc in enumerate((dk_acc, dv_acc)):
         factor = scale if index == 0 else 1.0
-        for step in (2, 1):
-            slot = index * 2 + step - 1
-            home_send[slot] = (acc[(2 - step) * 512 : (3 - step) * 512, :] * factor).astype(BF16)
-            homes.append(
-                send(
-                    home_send.at[slot],
-                    home_recv.at[slot],
-                    home_ss.at[slot],
-                    home_rs.at[slot],
-                    c_dev(-step),
-                )
+        slot = index * 2
+        home_send[slot] = (acc[512:1024, :] * factor).astype(BF16)
+        homes.append(
+            send(
+                home_send.at[slot],
+                home_recv.at[slot],
+                home_ss.at[index],
+                home_rs.at[index],
+                c_dev(-1),
             )
-
+        )
+
+    outs = []
+
+    def write(index, src, dst):
+        copy = pltpu.make_async_copy(src, dst, out_sem.at[index])
+        copy.start()
+        outs.append(copy)
+
+    write(0, dq_out, dq_hbm)
     sum_x(2)
     total_a = sum_x(3)
     for dz in (1, 2, 3):
         bz[dz].wait_recv()
 
-    def sum_z(dx):
-        rows = pl.ds(pl.multiple_of(((x + dx) % 4) * PIECE, 32), PIECE)
+    def sum_z(step):
+        rows = block_rows(step, 0, PIECE)
         total = stage[7, rows, :].astype(F32)
         for dz in (1, 2, 3):
             total = total + bz_recv[dz - 1, rows, :].astype(F32)
@@ -439,6 +516,7 @@
         for step in (1, 2):
             total = total + home_recv[index * 2 + step - 1].astype(F32)
         out[...] = total.astype(BF16)
+        write(1 + index, out, (dk_hbm, dv_hbm)[index])
 
     to_core[0].wait_recv()
     for n in range(4):
@@ -449,33 +527,64 @@
             + core_recv[0, :, cols].astype(F32)
             + y_recv[:, cols].astype(F32)
         ).astype(BF16)
+        write(3 + n, proj_out.at[:, cols], proj_hbm.at[:, cols])
 
     last.wait_recv()
     mine = jnp.where(lower, total_a, total_b)
     gw_out[...] = (mine + l_recv[...].astype(F32)) * (1.0 / 128.0)
+    write(7, gw_out, gw_hbm)
     for copy in sends:
         copy.wait_send()
+    for index in (0, 1):
+
+        @pl.when(x != 3)
+        def _():
+            near[index].wait_send()
+
+        @pl.when(x < 2)
+        def _():
+            far[index].wait_send()
+
+        @pl.when(x >= 2)
+        def _():
+            relays[index].wait_send()
+            hops[index][1].wait_send()
+
+        @pl.when(x == 3)
+        def _():
+            hops[index][0].wait_send()
+
+    for copy in outs:
+        copy.wait()
+
+
+def keep(*refs):
+    for src, dst in zip(refs[:5], refs[5:]):
+        dst[...] = src[...]
 
 
 def on_device(queries, keys, values, lengths, w_out, grad_y):
     hbm = pl.BlockSpec(memory_space=pl.ANY)
     vmem = pl.BlockSpec(memory_space=pltpu.VMEM)
-    dma = lambda n: pltpu.SemaphoreType.DMA((n,))
-    return pl.pallas_call(
-        kernel,
-        out_shape=(
+    dma = lambda *n: pltpu.SemaphoreType.DMA(n)
+    shapes = (
             jax.ShapeDtypeStruct((128, MODEL), BF16),
             jax.ShapeDtypeStruct((ROWS, COLS), BF16),
             jax.ShapeDtypeStruct((ROWS, E), BF16),
             jax.ShapeDtypeStruct((ROWS, E), BF16),
             jax.ShapeDtypeStruct((PIECE, COLS), F32),
-        ),
+    )
+    results = pl.pallas_call(
+        kernel,
+        out_shape=shapes,
         in_specs=[hbm, hbm, hbm, pl.BlockSpec(memory_space=pltpu.SMEM), hbm, hbm],
-        out_specs=(vmem,) * 5,
+        out_specs=(hbm,) * 5,
         scratch_shapes=[
+            *[pltpu.VMEM(s.shape, s.dtype) for s in shapes],
             pltpu.VMEM((ROWS, COLS), BF16),
             pltpu.VMEM((3 * ROWS, E), BF16),
             pltpu.VMEM((3 * ROWS, E), BF16),
+            pltpu.VMEM((2, ROWS, E), BF16),
             pltpu.VMEM((MODEL, COLS), BF16),
             pltpu.VMEM((ROWS, MODEL), BF16),
             pltpu.VMEM((ROWS, COLS), BF16),
@@ -501,7 +610,11 @@
             pltpu.VMEM((PIECE, COLS), BF16),
             pltpu.VMEM((PIECE, COLS), BF16),
             dma(5),
+            dma(8),
             dma(4),
+            dma(4),
+            dma(2),
+            dma(2),
             dma(4),
             dma(1),
             dma(1),
@@ -509,8 +622,10 @@
             dma(8),
             dma(8),
             dma(8),
-            dma(4),
-            dma(4),
+            dma(2),
+            dma(2),
+            dma(2, 4),
+            dma(2, 4),
             dma(2),
             dma(2),
             dma(4),
@@ -530,6 +645,9 @@
             collective_id=0, has_side_effects=True, vmem_limit_bytes=63 << 20
         ),
     )(queries, keys, values, lengths, w_out, grad_y)
+    return pl.pallas_call(
+        keep, out_shape=shapes, in_specs=[vmem] * 5, out_specs=(vmem,) * 5
+    )(*results)
 
 
 def solution(mesh):

time: 105 us -> 99.2 us (0.945)
  local copies, waits for them, and re-layouts: 5.59 us -> 0 us
    unnamed x13 -> x0, local copies, waits for them, and re-layouts: 5.59 us -> none
    pallas_call x1 -> x2, Pallas kernels: 98 us -> 98.1 us  [the longest x1 94.9 us: on_device(): pl.pallas_call(kernel, out_shape=shapes, in_specs=[hbm, hbm, hbm, pl.Bloc...]
where the time goes in v2:
time: 99.2 us; the launch traced here: 98.7 us
  Pallas kernels  98.1 us (99%)
    pallas_call x1, Pallas kernels, on_device(): pl.pallas_call(kernel, out_shape=shapes, in_specs=[hbm, hbm, hbm, pl.Bloc...  94.9 us
    pallas_call x1, Pallas kernels, on_device(): pl.pallas_call(keep, out_shape=shapes, in_specs=[vmem] * 5, out_specs=(vm...  3.21 us

profile of v2, /device:TPU:15, one launch (start us, length us, event | category | flops | bytes accessed | tf_op | source)
XLA Modules:
  0.0 98.7 jit_solution(6523994921107037513)
XLA Ops:
  0.6 94.9 %shard_map.101 = (bf16[128,5120]{1,0:T(8,128)(2,1)}, bf16[512,640]{1,0:T(8,128)(2,1)}, bf16[512,128]{1,0:T(8,128)(2,1)}, bf16[512,128]{1,0:T(8,128)(2,1)}, f32[160,640]{1,0:T(8,128)}) custom-call(bf16[512,640]{1,0:T(8,128)(2,1)} %q_hbm.1, bf16[512,128]{1,0:T(8,128)(2,1)} %k_hbm.1, bf16[512,128]{1,0:T(8,128)(2,1)} %v_hbm.1, s32[32]{0:T(128)} %lengths.1, ...), custom_call_target="tpu_custom_call" | custom-call | tf_op jit(solution)/shard_map/pallas_call | solution.py:577
  95.5 3.2 %shard_map.102 = (bf16[128,5120]{1,0:T(8,128)(2,1)}, bf16[512,640]{1,0:T(8,128)(2,1)}, bf16[512,128]{1,0:T(8,128)(2,1)}, bf16[512,128]{1,0:T(8,128)(2,1)}, f32[160,640]{1,0:T(8,128)}) custom-call(bf16[128,5120]{1,0:T(8,128)(2,1)} %get-tuple-element.10.refs_0_, bf16[512,640]{1,0:T(8,128)(2,1)} %get-tuple-element.11.refs_1_, ...), custom_call_target="tpu_custom_call" | custom-call | tf_op jit(solution)/shard_map/pallas_call | solution.py:648

commit v3 on v2

--- a/solution.py
+++ b/solution.py
@@ -76,6 +76,7 @@
     ax_recv,
     az_send,
     az_recv,
+    bz_relay,
     bz_recv,
     bx_send,
     bx_recv,
@@ -106,6 +107,8 @@
     ax_rs,
     az_ss,
     az_rs,
+    br_ss,
+    br_rs,
     bz_ss,
     bz_rs,
     bx_ss,
@@ -304,7 +307,7 @@
         ref = cot.at[far_rows, cols]
         forwards.append(send(ref, ref, fw_ss.at[n], fw_rs.at[n], core_dev))
 
-    ax, bz = {}, {}
+    ax, br, bz = {}, {}, {}
 
     def block_rows(step, first, count):
         return pl.ds(pl.multiple_of(((x + step) % 4) * PIECE + first, 16), count)
@@ -323,14 +326,33 @@
                     ax_rs.at[slot],
                     x_dev(dx),
                 )
-        elif step:
-            bz[step] = send(
-                stage.at[n],
-                bz_recv.at[step - 1],
-                bz_ss.at[step - 1],
-                bz_rs.at[step - 1],
-                z_dev(step),
-            )
+        elif step == 2:
+            for dx in Z_STEPS:
+                for way in (0, 1):
+                    slot = 2 * dx + way
+                    br[way, dx] = send(
+                        stage.at[n, block_rows(dx, 80 * way, 80)],
+                        bz_relay.at[slot],
+                        br_ss.at[slot],
+                        br_rs.at[slot],
+                        z_dev((1, 3)[way]),
+                    )
+
+    def relay_z(way, dx):
+        br[way, dx].wait_recv()
+        rows = block_rows(dx, 80 * way, 80)
+        slot = 2 * dx + way
+        stage[2 * way + 3, rows, :] = (
+            stage[2 * way + 3, rows, :].astype(F32) + bz_relay[slot].astype(F32)
+        ).astype(BF16)
+        whole = block_rows(dx, 0, PIECE)
+        bz[way, dx] = send(
+            stage.at[2 * way + 3, whole],
+            bz_recv.at[way, whole],
+            bz_ss.at[slot],
+            bz_rs.at[slot],
+            z_dev((1, 3)[way]),
+        )
 
     def raise_up(pair):
         first = pl.multiple_of(((z + Z_STEPS[pair]) % 4) * 2 * GROUP, 128)
@@ -359,12 +381,16 @@
         to_core[side] = send(
             part.at[rows_of(head)], core_recv.at[side], pc_ss.at[side], pc_rs.at[side], core_dev
         )
+    for n in range(4, 6):
+        forward(n)
     raise_up(0)
     raise_up(1)
-    for n in range(4, 6):
-        forward(n)
-    for n in range(4, 6):
+    for dx in Z_STEPS:
+        relay_z(0, dx)
+    for n in (5, 4):
         weight_group(n)
+    for dx in Z_STEPS:
+        relay_z(1, dx)
     to_core[1].wait_recv()
     to_far = []
 
@@ -405,6 +431,21 @@
             )
         return total
 
+    bx = {}
+
+    def sum_z(dx):
+        rows = block_rows(dx, 0, PIECE)
+        total = stage[7, rows, :].astype(F32)
+        for way in (0, 1):
+            bz[way, dx].wait_recv()
+            total = total + bz_recv[way, rows, :].astype(F32)
+        if dx:
+            bx_send[dx - 1] = total.astype(BF16)
+            bx[dx] = send(
+                bx_send.at[dx - 1], bx_recv.at[dx - 1], bx_ss.at[dx - 1], bx_rs.at[dx - 1], x_dev(dx)
+            )
+        return total
+
     sum_x(0)
 
     dk_acc[...] = jnp.zeros_like(dk_acc)
@@ -452,9 +493,17 @@
             dq_out[pl.ds(first, E), r * E : (r + 1) * E] = dq[:, r * E : (r + 1) * E].T.astype(BF16)
         return carry
 
-    lax.fori_loop(0, 2, backward, 0)
+    lax.fori_loop(0, 1, backward, 0)
     sum_x(1)
-    lax.fori_loop(2, 4, backward, 0)
+    lax.fori_loop(1, 2, backward, 0)
+    sum_z(2)
+    lax.fori_loop(2, 3, backward, 0)
+    sum_z(1)
+    sum_x(2)
+    lax.fori_loop(3, 4, backward, 0)
+    sum_z(3)
+    total_a = sum_x(3)
+    total_b = sum_z(0)
     homes = [home_piece(index, tile) for index in (0, 1) for tile in range(4)]
     sends.extend(homes)
     for index, acc in enumerate((dk_acc, dv_acc)):
@@ -479,25 +528,6 @@
         outs.append(copy)
 
     write(0, dq_out, dq_hbm)
-    sum_x(2)
-    total_a = sum_x(3)
-    for dz in (1, 2, 3):
-        bz[dz].wait_recv()
-
-    def sum_z(step):
-        rows = block_rows(step, 0, PIECE)
-        total = stage[7, rows, :].astype(F32)
-        for dz in (1, 2, 3):
-            total = total + bz_recv[dz - 1, rows, :].astype(F32)
-        return total
-
-    bx = {}
-    for dx in (2, 1, 3):
-        bx_send[dx - 1] = sum_z(dx).astype(BF16)
-        bx[dx] = send(
-            bx_send.at[dx - 1], bx_recv.at[dx - 1], bx_ss.at[dx - 1], bx_rs.at[dx - 1], x_dev(dx)
-        )
-    total_b = sum_z(0)
     for dz in (1, 2, 3):
         az[dz].wait_recv()
         total_a = total_a + az_recv[dz - 1].astype(F32)
@@ -604,7 +634,8 @@
             pltpu.VMEM((12, PIECE, COLS), BF16),
             pltpu.VMEM((3, PIECE, COLS), BF16),
             pltpu.VMEM((3, PIECE, COLS), BF16),
-            pltpu.VMEM((3, GROUP, COLS), BF16),
+            pltpu.VMEM((8, 80, COLS), BF16),
+            pltpu.VMEM((2, GROUP, COLS), BF16),
             pltpu.VMEM((3, PIECE, COLS), BF16),
             pltpu.VMEM((3, PIECE, COLS), BF16),
             pltpu.VMEM((PIECE, COLS), BF16),
@@ -634,8 +665,10 @@
             dma(12),
             dma(3),
             dma(3),
-            dma(3),
-            dma(3),
+            dma(8),
+            dma(8),
+            dma(8),
+            dma(8),
             dma(3),
             dma(3),
             dma(1),

time: 99.2 us -> 98.2 us (0.990)
  no operation moved by 1% of the time
where the time goes in v3:
time: 98.2 us; the launch traced here: 98.1 us
  Pallas kernels  97.4 us (99%)
    pallas_call x1, Pallas kernels, on_device(): pl.pallas_call(kernel, out_shape=shapes, in_specs=[hbm, hbm, hbm, pl.Bloc...  94.2 us
    pallas_call x1, Pallas kernels, on_device(): pl.pallas_call(keep, out_shape=shapes, in_specs=[vmem] * 5, out_specs=(vm...  3.21 us

profile of v3, /device:TPU:15, one launch (start us, length us, event | category | flops | bytes accessed | tf_op | source)
XLA Modules:
  0.0 98.1 jit_solution(17156597815103325649)
XLA Ops:
  0.6 94.2 %shard_map.101 = (bf16[128,5120]{1,0:T(8,128)(2,1)}, bf16[512,640]{1,0:T(8,128)(2,1)}, bf16[512,128]{1,0:T(8,128)(2,1)}, bf16[512,128]{1,0:T(8,128)(2,1)}, f32[160,640]{1,0:T(8,128)}) custom-call(bf16[512,640]{1,0:T(8,128)(2,1)} %q_hbm.1, bf16[512,128]{1,0:T(8,128)(2,1)} %k_hbm.1, bf16[512,128]{1,0:T(8,128)(2,1)} %v_hbm.1, s32[32]{0:T(128)} %lengths.1, ...), custom_call_target="tpu_custom_call" | custom-call | tf_op jit(solution)/shard_map/pallas_call | solution.py:607
  94.9 3.2 %shard_map.102 = (bf16[128,5120]{1,0:T(8,128)(2,1)}, bf16[512,640]{1,0:T(8,128)(2,1)}, bf16[512,128]{1,0:T(8,128)(2,1)}, bf16[512,128]{1,0:T(8,128)(2,1)}, f32[160,640]{1,0:T(8,128)}) custom-call(bf16[128,5120]{1,0:T(8,128)(2,1)} %get-tuple-element.10.refs_0_, bf16[512,640]{1,0:T(8,128)(2,1)} %get-tuple-element.11.refs_1_, ...), custom_call_target="tpu_custom_call" | custom-call | tf_op jit(solution)/shard_map/pallas_call | solution.py:681

commit v4 on v3

--- a/solution.py
+++ b/solution.py
@@ -678,8 +678,9 @@
             collective_id=0, has_side_effects=True, vmem_limit_bytes=63 << 20
         ),
     )(queries, keys, values, lengths, w_out, grad_y)
+    halves = tuple(pl.BlockSpec((s.shape[0] // 2, s.shape[1]), lambda i: (i, 0)) for s in shapes)
     return pl.pallas_call(
-        keep, out_shape=shapes, in_specs=[vmem] * 5, out_specs=(vmem,) * 5
+        keep, grid=(2,), out_shape=shapes, in_specs=list(halves), out_specs=halves
     )(*results)
 
 

time: 98.2 us -> 98 us (level)
  no operation moved by 1% of the time
where the time goes in v4:
time: 98 us; the launch traced here: 97.8 us
  Pallas kernels  97.1 us (99%)
    pallas_call x1, Pallas kernels, on_device(): pl.pallas_call(kernel, out_shape=shapes, in_specs=[hbm, hbm, hbm, pl.Bloc...  94.2 us
    pallas_call x1, Pallas kernels, on_device(): pl.pallas_call(keep, grid=(2,), out_shape=shapes, in_specs=list(halves),...  2.87 us

profile of v4, /device:TPU:15, one launch (start us, length us, event | category | flops | bytes accessed | tf_op | source)
XLA Modules:
  0.0 97.8 jit_solution(4474546767261527165)
XLA Ops:
  0.6 94.2 %shard_map.101 = (bf16[128,5120]{1,0:T(8,128)(2,1)}, bf16[512,640]{1,0:T(8,128)(2,1)}, bf16[512,128]{1,0:T(8,128)(2,1)}, bf16[512,128]{1,0:T(8,128)(2,1)}, f32[160,640]{1,0:T(8,128)}) custom-call(bf16[512,640]{1,0:T(8,128)(2,1)} %q_hbm.1, bf16[512,128]{1,0:T(8,128)(2,1)} %k_hbm.1, bf16[512,128]{1,0:T(8,128)(2,1)} %v_hbm.1, s32[32]{0:T(128)} %lengths.1, ...), custom_call_target="tpu_custom_call" | custom-call | tf_op jit(solution)/shard_map/pallas_call | solution.py:607
  94.9 2.9 %shard_map.102 = (bf16[128,5120]{1,0:T(8,128)(2,1)}, bf16[512,640]{1,0:T(8,128)(2,1)}, bf16[512,128]{1,0:T(8,128)(2,1)}, bf16[512,128]{1,0:T(8,128)(2,1)}, f32[160,640]{1,0:T(8,128)}) custom-call(bf16[128,5120]{1,0:T(8,128)(2,1)} %get-tuple-element.10.refs_0_, bf16[512,640]{1,0:T(8,128)(2,1)} %get-tuple-element.11.refs_1_, ...), custom_call_target="tpu_custom_call" | custom-call | tf_op jit(solution)/shard_map/pallas_call | solution.py:682
